TPU v7x, 256 devices: a whole 4x4x8 slice. The times are simulated.
256 devices in a mesh: blk: 64 (over y, z, x_lo), sub: 4 (over x_hi, core).
Axes of the slice: x: 4 (x_hi: 2, x_lo: 2; x = x_hi * 2 + x_lo), y: 4, z: 8, core: 2. Of those that a mesh axis runs over, the one named last changes fastest.
Arguments:
- tile_values: bfloat16 [2, 256, 128, 128, 128], P(None, ('blk', 'sub')), may hold values from -0.1875 to 0.1875
- tile_rows: int32 [2, 256, 128], P(None, ('blk', 'sub')), may hold values from 0 to 15
- tile_cols: int32 [2, 256, 128], P(None, ('blk', 'sub')), may hold values from 0 to 2047
- tile_counts: int32 [2, 256], P(None, ('blk', 'sub')), may hold values from 16 to 128, as said below
- labels: int32 [524288], P(('blk', 'sub')), may hold values from -1 to 1, as said below
- dual_logits: float32 [524288], P(('blk', 'sub')), may hold values from -6 to 6
- weights: float32 [16777216], P('blk'), may hold values from -6 to 6
- adagrad_sums: float32 [16777216], P('blk'), may hold values from 0.05 to 0.5
- section_steps: int32 [2], replicated, may hold values from 1 to 16
Outputs:
- weights_out: float32 [16777216], P('blk')
- adagrad_out: float32 [16777216], P('blk')
- dual_out: float32 [524288], P(('blk', 'sub'))
Inputs may be any that keep to these rules, and one draw needn't show every extreme that they name: `tile_counts`: slot k of a shard in a section holds a tile only when k is below its count; in every section some shard's count is 128. `labels`: each label is -1 or +1.
All inputs are finite; a program needn't handle non-finite values.
Results may differ from a plain program's by a relative error of at most 0.00067.
Values may be sent and summed in bfloat16 or wider, within the bound.
A program may use at most 64 MiB of HBM per device.

v0:
```python
import jax
import jax.numpy as jnp
from jax import lax
from jax.sharding import PartitionSpec as P

SECTIONS = 2


penalty = 0.1
dual_rate = 0.5
primal_rate = 0.8


def shifted(block, axis, distance):
    devices = range(lax.axis_size(axis))
    route = [((i - distance) % len(devices), i) for i in devices]
    return lax.ppermute(block, axis, route)


def shard_section(tile_block, row_ids, col_ids, filled, label_signs, logits, held_bf16, dual_step):
    tile_size = tile_block.shape[-1]
    row_tiles = logits.shape[0] // tile_size
    active = (jnp.arange(tile_block.shape[0], dtype=jnp.int32) < filled).astype(jnp.float32)
    columns = held_bf16.reshape(-1, tile_size)[col_ids]
    margin_tiles = jnp.einsum("kij,kj->ki", tile_block, columns, preferred_element_type=jnp.float32)
    onehot = (row_ids[:, None] == jnp.arange(row_tiles, dtype=jnp.int32)[None, :]).astype(
        jnp.float32
    ) * active[:, None]
    margins = jnp.dot(onehot.T, margin_tiles, precision=lax.Precision.HIGHEST).reshape(-1)
    logits = (1.0 - dual_step) * logits - dual_step * label_signs * margins
    scaled = (
        (jax.nn.sigmoid(logits) * label_signs).astype(jnp.bfloat16).reshape(row_tiles, tile_size)
    )
    backward = (
        jnp.einsum("kij,ki->kj", tile_block, scaled[row_ids], preferred_element_type=jnp.float32)
        * active[:, None]
    )
    partial_value = (
        jnp.zeros((held_bf16.shape[0] // tile_size, tile_size), jnp.float32)
        .at[col_ids]
        .add(backward)
    )
    return (logits, partial_value)


def per_device(
    tile_values,
    tile_rows,
    tile_cols,
    tile_counts,
    labels,
    dual_logits,
    weights,
    adagrad_sums,
    section_steps,
):
    label_signs = labels.astype(jnp.float32)
    logits = dual_logits
    held = weights
    sums = adagrad_sums
    for section_index in range(SECTIONS):
        steps_now = section_steps[section_index].astype(jnp.float32)
        dual_step = dual_rate / jnp.sqrt(steps_now)
        primal_step = primal_rate / jnp.sqrt(steps_now)
        held_bf16 = held.astype(jnp.bfloat16)
        logits, partial_value = shard_section(
            tile_values[section_index, 0],
            tile_rows[section_index, 0],
            tile_cols[section_index, 0],
            tile_counts[section_index, 0],
            label_signs,
            logits,
            held_bf16,
            dual_step,
        )
        gradient = penalty * held + lax.psum(partial_value, "sub").reshape(-1)
        sums = sums + gradient * gradient
        held = held - primal_step * gradient / jnp.sqrt(sums)
        moved = shifted(jnp.stack([held, sums]), "blk", 1)
        held = moved[0]
        sums = moved[1]
    return (held, sums, logits)


def solution(mesh):
    in_specs = (
        P(None, ("blk", "sub"), None, None, None),
        P(None, ("blk", "sub"), None),
        P(None, ("blk", "sub"), None),
        P(None, ("blk", "sub")),
        P(("blk", "sub")),
        P(("blk", "sub")),
        P("blk"),
        P("blk"),
        P(),
    )
    out_specs = (P("blk"), P("blk"), P(("blk", "sub")))
    return jax.shard_map(
        per_device, mesh=mesh, in_specs=in_specs, out_specs=out_specs, check_vma=False
    )
```

profile of v0, /device:TPU:1, one launch (start us, length us, event | category | flops | bytes accessed | tf_op | source)
XLA Modules:
  0.0 275.2 jit_solution(16171231967431805180)
XLA Ops:
  7.2 0.7 slice_bitcast_fusion
  7.9 0.7 fusion.41
  8.6 0.7 fusion.38
  9.3 1.4 fusion.45
  10.6 0.6 compare_convert_fusion.1
  11.3 1.3 fusion.46
  13.3 1.3 convert_bitcast_fusion
  14.6 0.7 gather_fusion
  15.4 4.4 %fusion.6 = f32[128,1,128]{2,1,0:T(1,128)S(1)} fusion(bf16[2,1,128,128,128]{4,3,2,1,0:T(8,128)(2,1)} %param.9, bf16[128,128,1]{1,0,2:T(8,128)(2,1)S(1)} %bitcast.84), kind=kOutput, calls=%fused_computation.12 | convolution fusion | flops 4194304 | bytes 4292608 | tf_op jit(solution)/shard_map/kij,kj->ki/dot_general | solution.py:25
  19.8 0.3 fusion.15
  20.2 0.7 gather_fusion.1
  20.9 3.4 %fusion.4 = f32[128,1,128]{2,1,0:T(1,128)S(1)} fusion(bf16[2,1,128,128,128]{4,3,2,1,0:T(8,128)(2,1)} %param.9, bf16[128,128,1]{1,0,2:T(8,128)(2,1)S(1)} %bitcast.85), kind=kOutput, calls=%fused_computation.10 | convolution fusion | flops 4194304 | bytes 4292608 | tf_op jit(solution)/shard_map/kij,ki->kj/dot_general | solution.py:35
  24.3 2.1 scatter_custom_fusion
  26.5 54.6 %all-reduce.3.cloned.1.call-done = f32[262144]{0:T(1024)} async-done(((f32[262144]{0:T(1024)}), f32[262144]{0:T(1024)}) %all-reduce.3.cloned.1.call-update) | async-done | bytes 1048592 | tf_op jit(solution)/shard_map/psum | solution.py:76
  81.1 1.5 multiply_subtract_fusion.1
  82.6 3.0 %pad_maximum_fusion = f32[2,262144]{1,0:T(2,128)} fusion(f32[1,262144]{1,0:T(1,128)S(1)} %bitcast.78, f32[1,262144]{1,0:T(1,128)S(1)} %bitcast.77), kind=kLoop, calls=%fused_computation.18 | loop fusion | flops 524288 | bytes 4194304 | tf_op jit(solution)/shard_map/stack | solution.py:79
  85.6 0.3 collective-permute-start
  86.6 0.7 compare_convert_fusion
  87.3 49.8 %collective-permute-done = f32[2,262144]{1,0:T(2,128)S(1)} collective-permute-done((f32[2,262144]{1,0:T(2,128)}, f32[2,262144]{1,0:T(2,128)S(1)}, u32[]{:S(2)}, u32[]{:S(2)}) %collective-permute-start) | collective-permute-done | bytes 2097184 | tf_op jit(solution)/shard_map/ppermute | solution.py:17
  137.1 10.9 %convert_reduce_fusion = bf16[262144]{0:T(1024)(128)(2,1)S(1)} fusion(f32[2,262144]{1,0:T(2,128)S(1)} %collective-permute-done), kind=kLoop, calls=%fused_computation.28 | loop fusion | bytes 1048576 | tf_op jit(solution)/shard_map/convert_element_type | solution.py:65
  148.0 0.7 gather_fusion.2
  148.7 4.4 %fusion.2 = f32[128,1,128]{2,1,0:T(1,128)S(1)} fusion(bf16[2,1,128,128,128]{4,3,2,1,0:T(8,128)(2,1)} %param.9, bf16[128,128,1]{1,0,2:T(8,128)(2,1)S(1)} %bitcast.86), kind=kOutput, calls=%fused_computation.8 | convolution fusion | flops 4194304 | bytes 4292608 | tf_op jit(solution)/shard_map/kij,kj->ki/dot_general | solution.py:25
  153.1 0.3 fusion.13
  153.5 0.7 gather_fusion.3
  154.2 3.4 %fusion = f32[128,1,128]{2,1,0:T(1,128)S(1)} fusion(bf16[2,1,128,128,128]{4,3,2,1,0:T(8,128)(2,1)} %param.9, bf16[128,128,1]{1,0,2:T(8,128)(2,1)S(1)} %bitcast.87), kind=kOutput, calls=%fused_computation.6 | convolution fusion | flops 4194304 | bytes 4292608 | tf_op jit(solution)/shard_map/kij,ki->kj/dot_general | solution.py:35
  157.6 2.1 scatter_custom_fusion.1
  159.7 48.9 %all-reduce.5.cloned.1.call-done = f32[1,262144]{1,0:T(1,128)} async-done(((f32[1,262144]{1,0:T(1,128)}), f32[1,262144]{1,0:T(1,128)}) %all-reduce.5.cloned.1.call-update) | async-done | bytes 1048592 | tf_op jit(solution)/shard_map/psum | solution.py:76
  208.6 3.8 %multiply_subtract_fusion = (f32[1,262144]{1,0:T(1,128)S(1)}, f32[1,262144]{1,0:T(1,128)S(1)}) fusion(f32[]{:T(128)} %bitcast.21, f32[1,262144]{1,0:T(1,128)} %all-reduce.5.cloned.1.call-done, f32[2,262144]{1,0:T(2,128)S(1)} %collective-permute-done), kind=kLoop, calls=%fused_computation.27 | loop fusion | flops 1835008 | bytes 5242884 | tf_op jit(solution)/shard_map/sub | solution.py:78
  212.4 1.9 pad_maximum_fusion.1
  214.4 0.4 collective-permute-start.1
  214.8 51.0 %collective-permute-done.1 = f32[2,262144]{1,0:T(2,128)S(1)} collective-permute-done((f32[2,262144]{1,0:T(2,128)S(1)}, f32[2,262144]{1,0:T(2,128)S(1)}, u32[]{:S(2)}, u32[]{:S(2)}) %collective-permute-start.1) | collective-permute-done | bytes 2097184 | tf_op jit(solution)/shard_map/ppermute | solution.py:17
  265.8 2.6 fusion.44
  (19 shorter events, 0.3 us)
Async XLA Ops:
  7.2 12.6 %copy-start.2 = (s32[2048]{0:T(1024)S(1)}, s32[2048]{0:T(1024)}, u32[]{:S(2)}) copy-start(s32[2048]{0:T(1024)} %param.13) | copy-start | bytes 24580
  7.2 12.6 %copy-start.4 = (f32[2048]{0:T(1024)S(1)}, f32[2048]{0:T(1024)}, u32[]{:S(2)}) copy-start(f32[2048]{0:T(1024)} %param.14) | copy-start | bytes 24580
  7.2 73.9 %all-reduce.3.cloned.1.call-start = ((), (), s32[]{:S(2)}) async-start(), calls=%async_computation | async-start | bytes 2097152 | tf_op jit(solution)/shard_map/psum | solution.py:76
  19.8 61.3 %copy-start = (f32[262144]{0:T(1024)S(1)}, f32[262144]{0:T(1024)}, u32[]{:S(2)}) copy-start(f32[262144]{0:T(1024)} %param.15) | copy-start | bytes 3145732
  19.8 61.3 %copy-start.1 = (f32[262144]{0:T(1024)S(1)}, f32[262144]{0:T(1024)}, u32[]{:S(2)}) copy-start(f32[262144]{0:T(1024)} %param.16) | copy-start | bytes 3145732
  26.4 182.2 %all-reduce.5.cloned.1.call-start = ((), (), s32[]{:S(2)}) async-start(), calls=%async_computation.1 | async-start | bytes 2097152 | tf_op jit(solution)/shard_map/psum | solution.py:76
  85.6 51.5 %collective-permute-start = (f32[2,262144]{1,0:T(2,128)}, f32[2,262144]{1,0:T(2,128)S(1)}, u32[]{:S(2)}, u32[]{:S(2)}) collective-permute-start(f32[2,262144]{1,0:T(2,128)} %pad_maximum_fusion), channel_id=1, source_target_pairs={{252,0},{0,4},{4,8},{8,12},{12,16},{16,20},{20,24},{24,28},{28,32}... | collective-permute-start | bytes 6291464 | tf_op jit(solution)/shard_map/ppermute | solution.py:17
  153.4 59.0 %copy-start.3 = (f32[2048]{0:T(1024)}, f32[2048]{0:T(1024)S(1)}, u32[]{:S(2)}) copy-start(f32[2048]{0:T(1024)S(1)} %fusion.13) | copy-start | bytes 24580
  214.4 51.4 %collective-permute-start.1 = (f32[2,262144]{1,0:T(2,128)S(1)}, f32[2,262144]{1,0:T(2,128)S(1)}, u32[]{:S(2)}, u32[]{:S(2)}) collective-permute-start(f32[2,262144]{1,0:T(2,128)S(1)} %pad_maximum_fusion.1), channel_id=1, source_target_pairs={{252,0},{0,4},{4,8},{8,12},{12,16},{16,20},{20,24},{24,28},{28,32}... | collective-permute-start | bytes 6291464 | tf_op jit(solution)/shard_map/ppermute | solution.py:17
Sparse Core Ops, SparseCore 0:
  26.5 54.5 all-reduce.2
  159.8 48.7 all-reduce.4
where the time goes:
time: 276 us; the launch traced here: 275 us
  waiting for transfers between devices  204 us (74%)
  local copies, waits for them, and re-layouts  19.7 us (7%)
  other arithmetic  18.4 us (7%)
  matrix products  16.2 us (6%)
  between operations  15.7 us (6%)
    psum x2, waiting for transfers between devices, per_device(): gradient = penalty * held + lax.psum(partial_value, 'sub').reshape(-1)  104 us
    ppermute x2, waiting for transfers between devices, shifted(): return lax.ppermute(block, axis, route)  101 us
    convert_element_type x1, local copies, waits for them, and re-layouts, per_device(): held_bf16 = held.astype(jnp.bfloat16)  10.9 us
    dot_general x2, matrix products, shard_section(): jnp.einsum('kij,kj->ki', tile_block, columns, preferred_element_type=jnp....  8.86 us
    dot_general x2, matrix products, shard_section(): jnp.einsum('kij,ki->kj', tile_block, scaled[row_ids], preferred_element_t...  6.74 us
  transfers between devices with their start and end apart: 4, of which 4 were waited for; matrix products, arithmetic and copies ran while one was open for 0% of the time, Pallas kernels for 0%

commit v1 on v0

v1 whole, which is shorter than its diff:
```python
import functools

import jax
import jax.numpy as jnp
from jax import lax
from jax.experimental import pallas as pl
from jax.experimental.pallas import tpu as pltpu
from jax.sharding import PartitionSpec as P

MESH = pl.DeviceIdType.MESH
SUBS = 4
SLOTS = 128
TILE = 128
GROUP = 16
GROUPS = SLOTS // GROUP
CTILES = 2048
HALF = CTILES // 2
PARTS = 4
PART = HALF // PARTS
GROWS = SLOTS + 8
OUT_PARTS = 8
OUT_PART = CTILES // OUT_PARTS

PENALTY = 0.1
DUAL_RATE = 0.5
PRIMAL_RATE = 0.8

F32 = jnp.float32
BF16 = jnp.bfloat16


def split_terms(value):
    high = value.astype(BF16)
    low = (value - high.astype(F32)).astype(BF16)
    return jnp.concatenate([high, low], axis=1)


def onehot_sum(match, terms):
    both = jnp.dot(match.astype(F32).astype(BF16), terms, preferred_element_type=F32)
    return both[:, :TILE] + both[:, TILE:]


def kernel(
    n,
    rows_s,
    cols_s,
    counts_s,
    steps_s,
    cols_v,
    labels_v,
    dual_v,
    tiles_h,
    weights_h,
    sums_h,
    weights_out,
    sums_out,
    dual_out,
    tiles,
    weights,
    sums,
    asked_v,
    asked_s,
    answer,
    answered,
    hrows,
    scaled,
    grads,
    near0,
    near1,
    far0,
    old,
    terms0,
    terms1,
    result,
    tile_sem,
    local_sem,
    ask_sem,
    asked_sem,
    answer_sem,
    dense_sem,
    copy_sem,
    grad_send,
    grad_recv,
    out_sem,
):
    p = lax.axis_index("blk")
    q = lax.axis_index("sub")
    core = lax.rem(q, 2)
    twin = q + 1 - 2 * core
    after = lax.rem(p + 1, n)
    after2 = lax.rem(p + 2, n)
    before = lax.rem(p + n - 1, n)
    before2 = lax.rem(p + n - 2, n)

    barrier = pltpu.get_barrier_semaphore()
    for other in range(SUBS):
        pl.semaphore_signal(barrier, inc=1, device_id=(before, other), device_id_type=MESH)
        pl.semaphore_signal(barrier, inc=1, device_id=(before2, other), device_id_type=MESH)
    pl.semaphore_signal(barrier, inc=1, device_id=(after, q), device_id_type=MESH)
    pl.semaphore_signal(barrier, inc=1, device_id=(p, twin), device_id_type=MESH)

    copy_w = pltpu.make_async_copy(weights_h, weights, local_sem.at[0])
    copy_w.start()
    for section in range(2):
        for g in range(GROUPS):
            pltpu.make_async_copy(
                tiles_h.at[section, 0, pl.ds(g * GROUP, GROUP)],
                tiles.at[section, pl.ds(g * GROUP, GROUP)],
                tile_sem.at[section, g],
            ).start()
        if section == 0:
            copy_s = pltpu.make_async_copy(sums_h, sums, local_sem.at[1])
            copy_s.start()

    pl.semaphore_wait(barrier, 2 * SUBS + 2)

    def remote(src, dst, send, recv, device):
        return pltpu.make_async_remote_copy(
            src_ref=src, dst_ref=dst, send_sem=send, recv_sem=recv, device_id=device, device_id_type=MESH
        )

    ask = remote(cols_v.at[1], asked_v, ask_sem.at[0], asked_sem.at[0], (before, q))
    ask.start()

    def dense(part, which):
        source = (weights_h, sums_h)[which]
        at = pl.multiple_of(core * HALF + part * PART, PART)
        return remote(
            source.at[pl.ds(at, PART)],
            old.at[which, pl.ds(at, PART)],
            dense_sem.at[0, which, part],
            dense_sem.at[1, which, part],
            (after2, q),
        )

    def forward_dense(part, which):
        at = pl.multiple_of(core * HALF + part * PART, PART)
        return remote(
            old.at[which, pl.ds(at, PART)],
            old.at[which, pl.ds(at, PART)],
            copy_sem.at[0, which, part],
            copy_sem.at[1, which, part],
            (p, twin),
        )

    for part in range(PARTS):
        for which in range(2):
            dense(part, which).start()

    sub16 = lax.broadcasted_iota(jnp.int32, (GROUP, TILE), 0)

    def section_pass(section, load_h, logits):
        count = counts_s[section]
        base = section * SLOTS

        def forward(g, total):
            pltpu.make_async_copy(
                tiles_h.at[section, 0, pl.ds(g * GROUP, GROUP)],
                tiles.at[section, pl.ds(g * GROUP, GROUP)],
                tile_sem.at[section, g],
            ).wait()
            for j in range(GROUP):
                k = g * GROUP + j
                row = jnp.where(k < count, rows_s[base + k], -1)
                lhs = jnp.where(sub16 == row, load_h(k), 0.0).astype(BF16)
                total = total + lax.dot_general(
                    lhs, tiles[section, k], (((1,), (1,)), ((), ())), preferred_element_type=F32
                )
            return total

        margins = lax.fori_loop(0, GROUPS, forward, jnp.zeros((GROUP, TILE), F32))
        steps = jnp.full((GROUP, TILE), steps_s[section], jnp.int32).astype(F32)
        dual_step = DUAL_RATE / jnp.sqrt(steps)
        signs = labels_v[...].astype(F32)
        logits = (1.0 - dual_step) * logits - dual_step * signs * margins
        scaled[...] = jax.nn.sigmoid(logits) * signs

        def backward(g, carry):
            total = jnp.zeros((GROUP, TILE), F32)
            for j in range(GROUP):
                k = g * GROUP + j
                slot = jnp.where(k < count, j, -1)
                value = scaled[pl.ds(rows_s[base + k], 1), :]
                lhs = jnp.where(sub16 == slot, value, 0.0).astype(BF16)
                total = total + jnp.dot(lhs, tiles[section, k], preferred_element_type=F32)
            grads[section, pl.ds(pl.multiple_of(g * GROUP, GROUP), GROUP), :] = total
            return carry

        lax.fori_loop(0, GROUPS, backward, 0)
        ids = jnp.broadcast_to(cols_v[section].astype(F32), (8, TILE))
        grads[section, pl.ds(SLOTS, 8), :] = ids
        return logits

    def send_grad(kind, other):
        section = (0, 1, 0)[kind]
        target = (near0, near1, far0)[kind]
        place = (after, after, after2)[kind]
        return remote(
            grads.at[section],
            target.at[q],
            grad_send.at[kind, other],
            grad_recv.at[kind, q],
            (place, other),
        )

    def recv_grad(kind, other):
        section = (0, 1, 0)[kind]
        target = (near0, near1, far0)[kind]
        return remote(
            grads.at[section], target.at[other], grad_send.at[kind, other], grad_recv.at[kind, other], (p, twin)
        )

    copy_w.wait()
    logits = section_pass(0, lambda k: weights[pl.ds(cols_s[k], 1), :], dual_v[...])
    for kind in (0, 2):
        for other in range(SUBS):
            send_grad(kind, other).start()

    ask.wait()
    to_scalar = pltpu.make_async_copy(asked_v, asked_s, local_sem.at[2])
    to_scalar.start()
    to_scalar.wait()
    copy_s.wait()

    def gather(g, carry):
        for j in range(GROUP):
            k = g * GROUP + j
            at = asked_s[0, k]
            answer[0, pl.ds(k, 1), :] = weights[pl.ds(at, 1), :]
            answer[1, pl.ds(k, 1), :] = sums[pl.ds(at, 1), :]
        return carry

    lax.fori_loop(0, GROUPS, gather, 0)
    give = remote(answer, answered, answer_sem.at[0], answer_sem.at[1], (after, q))
    give.start()

    def primal(section, shape):
        steps = jnp.full(shape, steps_s[section], jnp.int32).astype(F32)
        return PRIMAL_RATE / jnp.sqrt(steps)

    def fill_terms(terms, source):
        for other in range(SUBS):
            terms[pl.ds(other * SLOTS, SLOTS), :] = split_terms(source[other, :SLOTS, :])

    def lane_ids(source):
        return jnp.concatenate([source[other, SLOTS : SLOTS + 1, :] for other in range(SUBS)], axis=1)

    for other in range(SUBS):
        recv_grad(0, other).wait_recv()
    fill_terms(terms0, near0)
    mine = jnp.transpose(jnp.broadcast_to(cols_v[1].astype(F32), (TILE, TILE)))
    mine = jnp.concatenate([mine] * SUBS, axis=1)
    picked = onehot_sum(mine == lane_ids(near0), terms0[...])
    give.wait_recv()
    gradient = PENALTY * answered[0] + picked
    after_sums = answered[1] + gradient * gradient
    hrows[...] = answered[0] - primal(0, (SLOTS, TILE)) * gradient / jnp.sqrt(after_sums)

    logits = section_pass(1, lambda k: hrows[pl.ds(k, 1), :], logits)
    for other in range(SUBS):
        send_grad(1, other).start()
    dual_out[...] = logits

    for part in range(PARTS):
        for which in range(2):
            dense(part, which).wait_recv()
            forward_dense(part, which).start()
    for other in range(SUBS):
        recv_grad(2, other).wait_recv()
    fill_terms(terms0, far0)
    for other in range(SUBS):
        recv_grad(1, other).wait_recv()
    fill_terms(terms1, near1)
    for part in range(PARTS):
        for which in range(2):
            forward_dense(part, which).wait()

    def finish(part, carry):
        at = pl.multiple_of(part * OUT_PART, OUT_PART)
        ids = (lax.broadcasted_iota(jnp.int32, (OUT_PART, SUBS * SLOTS), 0) + at).astype(F32)
        w = old[0, pl.ds(at, OUT_PART), :]
        s = old[1, pl.ds(at, OUT_PART), :]
        g0 = PENALTY * w + onehot_sum(ids == lane_ids(far0), terms0[...])
        s = s + g0 * g0
        w = w - primal(0, (OUT_PART, TILE)) * g0 / jnp.sqrt(s)
        g1 = PENALTY * w + onehot_sum(ids == lane_ids(near1), terms1[...])
        s = s + g1 * g1
        w = w - primal(1, (OUT_PART, TILE)) * g1 / jnp.sqrt(s)
        result[0, pl.ds(at, OUT_PART), :] = w
        result[1, pl.ds(at, OUT_PART), :] = s
        pltpu.make_async_copy(
            result.at[0, pl.ds(at, OUT_PART)], weights_out.at[pl.ds(at, OUT_PART)], out_sem.at[0, part]
        ).start()
        pltpu.make_async_copy(
            result.at[1, pl.ds(at, OUT_PART)], sums_out.at[pl.ds(at, OUT_PART)], out_sem.at[1, part]
        ).start()
        return carry

    lax.fori_loop(0, OUT_PARTS, finish, 0)

    for part in range(PARTS):
        for which in range(2):
            dense(part, which).wait_send()
    for kind in range(3):
        for other in range(SUBS):
            send_grad(kind, other).wait_send()
    give.wait_send()

    def drain(part, carry):
        at = pl.multiple_of(part * OUT_PART, OUT_PART)
        pltpu.make_async_copy(
            result.at[0, pl.ds(at, OUT_PART)], weights_out.at[pl.ds(at, OUT_PART)], out_sem.at[0, part]
        ).wait()
        pltpu.make_async_copy(
            result.at[1, pl.ds(at, OUT_PART)], sums_out.at[pl.ds(at, OUT_PART)], out_sem.at[1, part]
        ).wait()
        return carry

    lax.fori_loop(0, OUT_PARTS, drain, 0)


def per_device(
    n, tile_values, tile_rows, tile_cols, tile_counts, labels, dual_logits, weights, adagrad_sums, section_steps
):
    any_space = pl.BlockSpec(memory_space=pl.ANY)
    smem = pl.BlockSpec(memory_space=pltpu.SMEM)
    vmem = pl.BlockSpec(memory_space=pltpu.VMEM)
    dma = pltpu.SemaphoreType.DMA
    out = pl.pallas_call(
        functools.partial(kernel, n),
        out_shape=(
            jax.ShapeDtypeStruct((CTILES, TILE), F32),
            jax.ShapeDtypeStruct((CTILES, TILE), F32),
            jax.ShapeDtypeStruct((GROUP, TILE), F32),
        ),
        in_specs=[smem, smem, smem, smem, vmem, vmem, vmem, any_space, any_space, any_space],
        out_specs=(any_space, any_space, vmem),
        scratch_shapes=[
            pltpu.VMEM((2, SLOTS, TILE, TILE), BF16),
            pltpu.VMEM((CTILES, TILE), F32),
            pltpu.VMEM((CTILES, TILE), F32),
            pltpu.VMEM((1, SLOTS), jnp.int32),
            pltpu.SMEM((1, SLOTS), jnp.int32),
            pltpu.VMEM((2, SLOTS, TILE), F32),
            pltpu.VMEM((2, SLOTS, TILE), F32),
            pltpu.VMEM((SLOTS, TILE), F32),
            pltpu.VMEM((GROUP, TILE), F32),
            pltpu.VMEM((2, GROWS, TILE), F32),
            pltpu.VMEM((SUBS, GROWS, TILE), F32),
            pltpu.VMEM((SUBS, GROWS, TILE), F32),
            pltpu.VMEM((SUBS, GROWS, TILE), F32),
            pltpu.VMEM((2, CTILES, TILE), F32),
            pltpu.VMEM((SUBS * SLOTS, 2 * TILE), BF16),
            pltpu.VMEM((SUBS * SLOTS, 2 * TILE), BF16),
            pltpu.VMEM((2, CTILES, TILE), F32),
            dma((2, GROUPS)),
            dma((3,)),
            dma((1,)),
            dma((1,)),
            dma((2,)),
            dma((2, 2, PARTS)),
            dma((2, 2, PARTS)),
            dma((3, SUBS)),
            dma((3, SUBS)),
            dma((2, OUT_PARTS)),
        ],
        compiler_params=pltpu.CompilerParams(
            collective_id=0, has_side_effects=True, vmem_limit_bytes=62 * 1024 * 1024
        ),
        name="descent",
    )(
        tile_rows.reshape(-1),
        tile_cols.reshape(-1),
        tile_counts.reshape(-1),
        section_steps,
        tile_cols,
        labels.reshape(GROUP, TILE),
        dual_logits.reshape(GROUP, TILE),
        tile_values,
        weights.reshape(CTILES, TILE),
        adagrad_sums.reshape(CTILES, TILE),
    )
    return out[0].reshape(-1), out[1].reshape(-1), out[2].reshape(-1)


def solution(mesh):
    in_specs = (
        P(None, ("blk", "sub"), None, None, None),
        P(None, ("blk", "sub"), None),
        P(None, ("blk", "sub"), None),
        P(None, ("blk", "sub")),
        P(("blk", "sub")),
        P(("blk", "sub")),
        P("blk"),
        P("blk"),
        P(),
    )
    out_specs = (P("blk"), P("blk"), P(("blk", "sub")))
    return jax.shard_map(
        functools.partial(per_device, mesh.shape["blk"]),
        mesh=mesh,
        in_specs=in_specs,
        out_specs=out_specs,
        check_vma=False,
    )
```

time: 276 us -> 73.4 us (0.27)
  waiting for transfers between devices: 204 us -> 0 us
  Pallas kernels: 0 us -> 65.4 us
  other arithmetic: 18.4 us -> 0 us
  matrix products: 16.2 us -> 0 us
  between operations: 15.7 us -> 0.64 us
  local copies, waits for them, and re-layouts: 19.7 us -> 5.82 us
    psum x2 -> x0, waiting for transfers between devices: 104 us -> none  [per_device(): gradient = penalty * held + lax.psum(partial_value, 'sub').reshape(-1)]
    ppermute x2 -> x0, waiting for transfers between devices: 101 us -> none  [shifted(): return lax.ppermute(block, axis, route)]
    pallas_call x0 -> x1, Pallas kernels: none -> 65.4 us  [per_device(): pl.pallas_call(functools.partial(kernel, n), out_shape=(jax.ShapeDtypeStr...]
    dot_general x6 -> x0, matrix products: 16.2 us -> none  [the longest x2 8.86 us: shard_section(): jnp.einsum('kij,kj->ki', tile_block, columns, preferred_element_type=jnp....]
    convert_element_type x1 -> x0, local copies, waits for them, and re-layouts: 10.9 us -> none  [per_device(): held_bf16 = held.astype(jnp.bfloat16)]
    unnamed x10 -> x3, local copies, waits for them, and re-layouts: 0.05 us -> 5.82 us
    sub x2 -> x0, other arithmetic: 5.31 us -> none  [per_device(): held = held - primal_step * gradient / jnp.sqrt(sums)]
    slice x3 -> x0, local copies, waits for them, and re-layouts: 5.29 us -> none  [the longest x1 2.6 us: per_device(): sums = moved[1]]
  transfers between devices with their start and end apart: 4 -> 0, of which waited for: 4 -> 0; matrix products, arithmetic and copies ran while one was open for 0% -> 0% of each run, Pallas kernels for 0% -> 0%
where the time goes in v1:
time: 73.4 us; the launch traced here: 71.9 us
  Pallas kernels  65.4 us (89%)
  local copies, waits for them, and re-layouts  5.82 us (8%)
    pallas_call x1, Pallas kernels, per_device(): pl.pallas_call(functools.partial(kernel, n), out_shape=(jax.ShapeDtypeStr...  65.4 us
    unnamed x3, local copies, waits for them, and re-layouts  5.82 us

profile of v1, /device:TPU:1, one launch (start us, length us, event | category | flops | bytes accessed | tf_op | source)
XLA Modules:
  0.0 71.9 jit_solution(13190648431516994431)
XLA Ops:
  0.6 65.4 %descent.1 = (f32[2048,128]{1,0:T(8,128)}, f32[2048,128]{1,0:T(8,128)}, f32[16,128]{1,0:T(8,128)}) custom-call(s32[256]{0:T(256)} %bitcast.18, s32[256]{0:T(256)} %bitcast.17, s32[2]{0:T(128)} %bitcast.19, s32[2]{0:T(128)} %steps_s.1, s32[2,1,128]{2,1,0:T(1,128)} %cols_v.1, s32[16,128]{1,0:T(8,128)} %bitcast.14, f32[16,128]{1,0:T(8,128)} %bitcast.15, ...), custom_call_target="tpu_custom_call" | custom-call | tf_op jit(solution)/shard_map/descent/pallas_call | solution.py:329
  66.1 2.3 %copy.15 = f32[262144]{0:T(1024)} copy(f32[262144]{0:T(1024)} %bitcast.13) | data formatting | bytes 2097152
  68.3 2.3 %copy.16 = f32[262144]{0:T(1024)} copy(f32[262144]{0:T(1024)} %bitcast.12) | data formatting | bytes 2097152
  70.6 1.3 %copy.17 = f32[2048]{0:T(1024)} copy(f32[2048]{0:T(1024)} %bitcast.16) | data formatting | bytes 16384

commit v2 on v1

v2 whole, which is shorter than its diff:
```python
import functools

import jax
import jax.numpy as jnp
from jax import lax
from jax.experimental import pallas as pl
from jax.experimental.pallas import tpu as pltpu
from jax.sharding import PartitionSpec as P

MESH = pl.DeviceIdType.MESH
SUBS = 4
SLOTS = 128
TILE = 128
GROUP = 16
GROUPS = SLOTS // GROUP
WIDE = 4
CTILES = 2048
QUARTER = CTILES // SUBS
PIECES = 2
PIECE = QUARTER // PIECES
GROWS = SLOTS + 8
CROWS = SLOTS + GROUP
OUT_PARTS = SUBS
OUT_PART = CTILES // OUT_PARTS
LOADS = (4, 2)

PENALTY = 0.1
DUAL_RATE = 0.5
PRIMAL_RATE = 0.8

LEVELS = 32766.0
WEIGHT_CODE = (-25.0, 27.6)
GRADIENT_CODE = (-18.0, 22.7)
SUM_MID = 0.275
SUM_SCALE = 32767.0 / 0.22501

F32 = jnp.float32
BF16 = jnp.bfloat16
I32 = jnp.int32


def encode_log(value, code_range):
    low, span = code_range
    size = jnp.log2(jnp.maximum(jnp.abs(value), 1e-30))
    code = jnp.clip(jnp.round((size - low) * (LEVELS / span)), 0.0, LEVELS)
    return jnp.where(value < 0.0, -code, code).astype(I32).astype(jnp.int16)


def decode_log(code, code_range):
    low, span = code_range
    code = code.astype(I32).astype(F32)
    size = jnp.exp2(jnp.abs(code) * (span / LEVELS) + low)
    return jnp.where(code < 0.0, -size, jnp.where(code > 0.0, size, 0.0))


def encode_sums(value):
    code = jnp.clip(jnp.round((value - SUM_MID) * SUM_SCALE), -32767.0, 32767.0)
    return code.astype(I32).astype(jnp.int16)


def decode_sums(code):
    return code.astype(I32).astype(F32) * (1.0 / SUM_SCALE) + SUM_MID


def split_terms(value):
    high = value.astype(BF16)
    low = (value - high.astype(F32)).astype(BF16)
    return jnp.concatenate([high, low], axis=1)


def onehot_sum(match, terms):
    both = jnp.dot(match.astype(F32).astype(BF16), terms, preferred_element_type=F32)
    return both[:, :TILE] + both[:, TILE:]


def fill_terms(terms, source, coded):
    for other in range(SUBS):
        value = source[other, :SLOTS, :]
        if coded:
            value = decode_log(value, GRADIENT_CODE)
        terms[pl.ds(other * SLOTS, SLOTS), :] = split_terms(value)


def lane_ids(source, coded):
    ids = [source[other, SLOTS:, :] for other in range(SUBS)]
    if coded:
        ids = [value.astype(I32).astype(F32) for value in ids]
    return jnp.concatenate([value[:1, :] for value in ids], axis=1)


def primal_step(steps_s, section, shape):
    steps = jnp.full(shape, steps_s[section], I32).astype(F32)
    return PRIMAL_RATE / jnp.sqrt(steps)


def part_ids(at):
    return (lax.broadcasted_iota(I32, (OUT_PART, SUBS * SLOTS), 0) + at).astype(F32)


def kernel(
    n,
    rows_s,
    cols_s,
    counts_s,
    steps_s,
    cols_v,
    labels_v,
    dual_v,
    tiles_h,
    weights_h,
    sums_h,
    mid_weights,
    mid_sums,
    near1,
    dual_out,
    tiles,
    weights,
    sums,
    asked_v,
    asked_s,
    answer,
    answered,
    hrows,
    scaled,
    grads,
    coded,
    near0,
    far0,
    codes,
    old,
    terms,
    result,
    tile_sem,
    local_sem,
    ask_sem,
    answer_sem,
    dense_send,
    dense_recv,
    grad_send,
    grad_recv,
    out_sem,
):
    p = lax.axis_index("blk")
    q = lax.axis_index("sub")
    twin = q + 1 - 2 * lax.rem(q, 2)
    opp = lax.rem(q + 2, SUBS)
    opptwin = lax.rem(twin + 2, SUBS)
    after = lax.rem(p + 1, n)
    after2 = lax.rem(p + 2, n)
    before = lax.rem(p + n - 1, n)
    before2 = lax.rem(p + n - 2, n)

    barrier = pltpu.get_barrier_semaphore()
    senders = [(before, q), (before, opp), (before2, q), (before2, opp), (after, q), (p, twin), (p, opp)]
    for device in senders:
        pl.semaphore_signal(barrier, inc=1, device_id=device, device_id_type=MESH)

    def tile_copy(section, load):
        size = SLOTS // LOADS[section]
        return pltpu.make_async_copy(
            tiles_h.at[section, 0, pl.ds(load * size, size)],
            tiles.at[section, pl.ds(load * size, size)],
            tile_sem.at[section, load],
        )

    copy_w = pltpu.make_async_copy(weights_h, weights, local_sem.at[0])
    copy_w.start()
    for load in range(LOADS[0]):
        tile_copy(0, load).start()
    copy_s = pltpu.make_async_copy(sums_h, sums, local_sem.at[1])
    copy_s.start()
    for load in range(LOADS[1]):
        tile_copy(1, load).start()

    def remote(src, dst, send, recv, device):
        return pltpu.make_async_remote_copy(
            src_ref=src, dst_ref=dst, send_sem=send, recv_sem=recv, device_id=device, device_id_type=MESH
        )

    sub16 = lax.broadcasted_iota(I32, (GROUP, TILE), 0)

    def forward(section, load_h):
        count = counts_s[section]
        base = section * SLOTS

        def group(g, total):
            for j in range(0, GROUP, WIDE):
                lhs = []
                for i in range(WIDE):
                    k = g * GROUP + j + i
                    row = jnp.where(k < count, rows_s[base + k], -1)
                    lhs.append(jnp.where(sub16 == row, load_h(k), 0.0).astype(BF16))
                rhs = [tiles[section, g * GROUP + j + i] for i in range(WIDE)]
                total = total + lax.dot_general(
                    jnp.concatenate(lhs, axis=1),
                    jnp.concatenate(rhs, axis=1),
                    (((1,), (1,)), ((), ())),
                    preferred_element_type=F32,
                )
            return total

        total = jnp.zeros((GROUP, TILE), F32)
        each = GROUPS // LOADS[section]
        for load in range(LOADS[section]):
            tile_copy(section, load).wait()
            total = lax.fori_loop(load * each, (load + 1) * each, group, total)
        return total

    def new_logits(section, logits, margins):
        steps = jnp.full((GROUP, TILE), steps_s[section], I32).astype(F32)
        dual_step = DUAL_RATE / jnp.sqrt(steps)
        signs = labels_v[...].astype(F32)
        logits = (1.0 - dual_step) * logits - dual_step * signs * margins
        scaled[...] = jax.nn.sigmoid(logits) * signs
        return logits

    def backward(section):
        count = counts_s[section]
        base = section * SLOTS

        def group(g, carry):
            lhs = []
            for j in range(GROUP):
                k = g * GROUP + j
                slot = jnp.where(k < count, j, -1)
                value = scaled[pl.ds(rows_s[base + k], 1), :]
                lhs.append(jnp.where(sub16 == slot, value, 0.0).astype(BF16))
            rhs = tiles[section, pl.ds(g * GROUP, GROUP)].reshape(GROUP * TILE, TILE)
            grads[section, pl.ds(pl.multiple_of(g * GROUP, GROUP), GROUP), :] = jnp.dot(
                jnp.concatenate(lhs, axis=1), rhs, preferred_element_type=F32
            )
            return carry

        lax.fori_loop(0, GROUPS, group, 0)

    ask = remote(cols_v.at[1], asked_v, ask_sem.at[0], ask_sem.at[1], (before, q))

    def dense(stage, piece):
        owner = opp if stage == 3 else q
        to = ((after2, q), (p, opp), (p, twin), (p, twin))[stage]
        src = codes.at[piece] if stage == 0 else old.at[owner, piece]
        return remote(src, old.at[owner, piece], dense_send.at[stage, piece], dense_recv.at[stage, piece], to)

    def dense_arrived(stage, piece):
        ref = old.at[(q, opp, twin, opptwin)[stage], piece]
        remote(ref, ref, dense_send.at[stage, piece], dense_recv.at[stage, piece], (p, twin)).wait_recv()

    def grad(kind, stage, way):
        target = (near0, near1, far0)[kind]
        owner = (q, opp)[way]
        if stage == 0:
            src, slot = (grads.at[0], coded.at[1], coded.at[0])[kind], q
            to = ((after, after, after2)[kind], owner)
        else:
            src, slot = target.at[owner], owner
            to = (p, twin)
        return remote(
            src, target.at[slot], grad_send.at[kind, stage, way], grad_recv.at[kind, stage, way], to
        )

    def grad_arrived(kind, stage, way):
        target = (near0, near1, far0)[kind]
        owner = ((q, opp), (twin, opptwin))[stage][way]
        ref = target.at[owner]
        remote(
            ref, ref, grad_send.at[kind, stage, way], grad_recv.at[kind, stage, way], (p, twin)
        ).wait_recv()

    grads[0, pl.ds(SLOTS, 8), :] = jnp.broadcast_to(cols_v[0].astype(F32), (8, TILE))
    for section in range(2):
        coded[section, pl.ds(SLOTS, GROUP), :] = jnp.broadcast_to(cols_v[section], (GROUP, TILE)).astype(
            jnp.int16
        )

    copy_w.wait()
    margins = forward(0, lambda k: weights[pl.ds(cols_s[k], 1), :])
    logits = new_logits(0, dual_v[...], margins)

    pl.semaphore_wait(barrier, len(senders))
    ask.start()
    backward(0)
    for way in range(2):
        grad(0, 0, way).start()

    copy_s.wait()
    for piece in range(PIECES):
        at = pl.multiple_of(q * QUARTER + piece * PIECE, PIECE)
        codes[piece, 0] = encode_log(weights[pl.ds(at, PIECE), :], WEIGHT_CODE)
        codes[piece, 1] = encode_sums(sums[pl.ds(at, PIECE), :])
    coded[0, :SLOTS, :] = encode_log(grads[0, :SLOTS, :], GRADIENT_CODE)

    ask.wait()
    to_scalar = pltpu.make_async_copy(asked_v, asked_s, local_sem.at[2])
    to_scalar.start()
    to_scalar.wait()

    def gather(g, carry):
        for j in range(GROUP):
            k = g * GROUP + j
            at = asked_s[0, k]
            answer[0, pl.ds(k, 1), :] = weights[pl.ds(at, 1), :]
            answer[1, pl.ds(k, 1), :] = sums[pl.ds(at, 1), :]
        return carry

    lax.fori_loop(0, GROUPS, gather, 0)
    give = remote(answer, answered, answer_sem.at[0], answer_sem.at[1], (after, q))
    give.start()
    for piece in range(PIECES):
        dense(0, piece).start()
    for way in range(2):
        grad(2, 0, way).start()

    mine = jnp.transpose(jnp.broadcast_to(cols_v[1].astype(F32), (TILE, TILE)))
    mine = jnp.concatenate([mine] * SUBS, axis=1)
    for way in range(2):
        grad_arrived(0, 0, way)
        grad(0, 1, way).start()
    give.wait_recv()
    for way in range(2):
        grad_arrived(0, 1, way)
    fill_terms(terms, near0, False)
    picked = onehot_sum(mine == lane_ids(near0, False), terms[...])
    gradient = PENALTY * answered[0] + picked
    after_sums = answered[1] + gradient * gradient
    hrows[...] = answered[0] - primal_step(steps_s, 0, (SLOTS, TILE)) * gradient / jnp.sqrt(after_sums)

    margins = forward(1, lambda k: hrows[pl.ds(k, 1), :])
    logits = new_logits(1, logits, margins)
    dual_out[...] = logits
    dense_arrived(0, 0)
    dense(1, 0).start()
    dense(2, 0).start()
    backward(1)
    coded[1, :SLOTS, :] = encode_log(grads[1, :SLOTS, :], GRADIENT_CODE)
    for way in range(2):
        grad(1, 0, way).start()

    for piece in range(1, PIECES):
        dense_arrived(0, piece)
        dense(1, piece).start()
        dense(2, piece).start()
    for way in range(2):
        grad_arrived(2, 0, way)
        grad(2, 1, way).start()
    dense_arrived(1, 0)
    dense(3, 0).start()
    for way in range(2):
        grad_arrived(2, 1, way)
    fill_terms(terms, far0, True)
    ids0 = lane_ids(far0, True)

    def mid_copy(owner, which):
        at = pl.multiple_of(owner * OUT_PART, OUT_PART)
        return pltpu.make_async_copy(
            result.at[which, pl.ds(at, OUT_PART)],
            (mid_weights, mid_sums)[which].at[pl.ds(at, OUT_PART)],
            out_sem.at[which, owner],
        )

    def section0(owner):
        at = pl.multiple_of(owner * OUT_PART, OUT_PART)
        w = decode_log(old[owner, :, 0].reshape(OUT_PART, TILE), WEIGHT_CODE)
        s = decode_sums(old[owner, :, 1].reshape(OUT_PART, TILE))
        gradient = PENALTY * w + onehot_sum(part_ids(at) == ids0, terms[...])
        s = s + gradient * gradient
        result[0, pl.ds(at, OUT_PART), :] = (
            w - primal_step(steps_s, 0, (OUT_PART, TILE)) * gradient / jnp.sqrt(s)
        )
        result[1, pl.ds(at, OUT_PART), :] = s
        for which in range(2):
            mid_copy(owner, which).start()

    section0(q)
    for piece in range(PIECES):
        dense_arrived(2, piece)
    section0(twin)
    for piece in range(1, PIECES):
        dense_arrived(1, piece)
        dense(3, piece).start()
    for way in range(2):
        grad_arrived(1, 0, way)
        grad(1, 1, way).start()
    section0(opp)
    for piece in range(PIECES):
        dense_arrived(3, piece)
    section0(opptwin)

    for way in range(2):
        grad_arrived(1, 1, way)

    for stage in range(4):
        for piece in range(PIECES):
            dense(stage, piece).wait_send()
    for kind in range(3):
        for stage in range(2):
            for way in range(2):
                grad(kind, stage, way).wait_send()
    give.wait_send()
    for owner in range(SUBS):
        for which in range(2):
            mid_copy(owner, which).wait()


def finish_kernel(
    steps_s, dual_in, mid_weights, mid_sums, near, weights_out, sums_out, dual_out, terms, result, out_sem
):
    def out_copy(part, which):
        at = part * OUT_PART
        return pltpu.make_async_copy(
            result.at[which, pl.ds(at, OUT_PART)],
            (weights_out, sums_out)[which].at[pl.ds(at, OUT_PART)],
            out_sem.at[which, part],
        )

    dual_out[...] = dual_in[...]
    fill_terms(terms, near, True)
    ids1 = lane_ids(near, True)
    for part in range(OUT_PARTS):
        at = part * OUT_PART
        w = mid_weights[pl.ds(at, OUT_PART), :]
        gradient = PENALTY * w + onehot_sum(part_ids(at) == ids1, terms[...])
        s = mid_sums[pl.ds(at, OUT_PART), :] + gradient * gradient
        result[0, pl.ds(at, OUT_PART), :] = (
            w - primal_step(steps_s, 1, (OUT_PART, TILE)) * gradient / jnp.sqrt(s)
        )
        result[1, pl.ds(at, OUT_PART), :] = s
        for which in range(2):
            out_copy(part, which).start()
    for part in range(OUT_PARTS):
        for which in range(2):
            out_copy(part, which).wait()


def per_device(
    n, tile_values, tile_rows, tile_cols, tile_counts, labels, dual_logits, weights, adagrad_sums, section_steps
):
    any_space = pl.BlockSpec(memory_space=pl.ANY)
    smem = pl.BlockSpec(memory_space=pltpu.SMEM)
    vmem = pl.BlockSpec(memory_space=pltpu.VMEM)
    dma = pltpu.SemaphoreType.DMA
    dense_shape = jax.ShapeDtypeStruct((CTILES, TILE), F32)
    row_shape = jax.ShapeDtypeStruct((GROUP, TILE), F32)
    mid_weights, mid_sums, near1, dual = pl.pallas_call(
        functools.partial(kernel, n),
        out_shape=(dense_shape, dense_shape, jax.ShapeDtypeStruct((SUBS, CROWS, TILE), jnp.int16), row_shape),
        in_specs=[smem, smem, smem, smem, vmem, vmem, vmem, any_space, any_space, any_space],
        out_specs=(any_space, any_space, any_space, vmem),
        scratch_shapes=[
            pltpu.VMEM((2, SLOTS, TILE, TILE), BF16),
            pltpu.VMEM((CTILES, TILE), F32),
            pltpu.VMEM((CTILES, TILE), F32),
            pltpu.VMEM((1, SLOTS), I32),
            pltpu.SMEM((1, SLOTS), I32),
            pltpu.VMEM((2, SLOTS, TILE), F32),
            pltpu.VMEM((2, SLOTS, TILE), F32),
            pltpu.VMEM((SLOTS, TILE), F32),
            pltpu.VMEM((GROUP, TILE), F32),
            pltpu.VMEM((2, GROWS, TILE), F32),
            pltpu.VMEM((2, CROWS, TILE), jnp.int16),
            pltpu.VMEM((SUBS, GROWS, TILE), F32),
            pltpu.VMEM((SUBS, CROWS, TILE), jnp.int16),
            pltpu.VMEM((PIECES, 2, PIECE, TILE), jnp.int16),
            pltpu.VMEM((SUBS, PIECES, 2, PIECE, TILE), jnp.int16),
            pltpu.VMEM((SUBS * SLOTS, 2 * TILE), BF16),
            pltpu.VMEM((2, CTILES, TILE), F32),
            dma((2, max(LOADS))),
            dma((3,)),
            dma((2,)),
            dma((2,)),
            dma((4, PIECES)),
            dma((4, PIECES)),
            dma((3, 2, 2)),
            dma((3, 2, 2)),
            dma((2, OUT_PARTS)),
        ],
        compiler_params=pltpu.CompilerParams(
            collective_id=0, has_side_effects=True, vmem_limit_bytes=62 * 1024 * 1024
        ),
        name="descent",
    )(
        tile_rows.reshape(-1),
        tile_cols.reshape(-1),
        tile_counts.reshape(-1),
        section_steps,
        tile_cols,
        labels.reshape(GROUP, TILE),
        dual_logits.reshape(GROUP, TILE),
        tile_values,
        weights.reshape(CTILES, TILE),
        adagrad_sums.reshape(CTILES, TILE),
    )
    out = pl.pallas_call(
        finish_kernel,
        out_shape=(dense_shape, dense_shape, row_shape),
        in_specs=[smem, vmem, vmem, vmem, vmem],
        out_specs=(any_space, any_space, vmem),
        scratch_shapes=[
            pltpu.VMEM((SUBS * SLOTS, 2 * TILE), BF16),
            pltpu.VMEM((2, CTILES, TILE), F32),
            dma((2, OUT_PARTS)),
        ],
        compiler_params=pltpu.CompilerParams(vmem_limit_bytes=62 * 1024 * 1024),
        name="finish",
    )(section_steps, dual, mid_weights, mid_sums, near1)
    return out[0].reshape(-1), out[1].reshape(-1), out[2].reshape(-1)


def solution(mesh):
    in_specs = (
        P(None, ("blk", "sub"), None, None, None),
        P(None, ("blk", "sub"), None),
        P(None, ("blk", "sub"), None),
        P(None, ("blk", "sub")),
        P(("blk", "sub")),
        P(("blk", "sub")),
        P("blk"),
        P("blk"),
        P(),
    )
    out_specs = (P("blk"), P("blk"), P(("blk", "sub")))
    return jax.shard_map(
        functools.partial(per_device, mesh.shape["blk"]),
        mesh=mesh,
        in_specs=in_specs,
        out_specs=out_specs,
        check_vma=False,
    )
```

time: 73.4 us -> 48.3 us (0.66); the launches traced: 71.9 us -> 48.2 us
  Pallas kernels: 65.4 us -> 47.5 us
  local copies, waits for them, and re-layouts: 5.82 us -> 0 us
    pallas_call x1 -> x2, Pallas kernels: 65.4 us -> 47.5 us  [the longest x1 43.1 us: per_device(): pl.pallas_call(functools.partial(kernel, n), out_shape=(dense_shape, dens...]
    unnamed x3 -> x0, local copies, waits for them, and re-layouts: 5.82 us -> none
where the time goes in v2:
time: 48.3 us; the launch traced here: 48.2 us
  Pallas kernels  47.5 us (98%)
  between operations  0.64 us (1%)
    pallas_call x1, Pallas kernels, per_device(): pl.pallas_call(functools.partial(kernel, n), out_shape=(dense_shape, dens...  43.1 us
    pallas_call x1, Pallas kernels, per_device(): pl.pallas_call(finish_kernel, out_shape=(dense_shape, dense_shape, row_sh...  4.39 us

profile of v2, /device:TPU:1, one launch (start us, length us, event | category | flops | bytes accessed | tf_op | source)
XLA Modules:
  0.0 48.2 jit_solution(6866496869645703078)
XLA Ops:
  0.6 43.1 %descent.1 = (f32[2048,128]{1,0:T(8,128)}, f32[2048,128]{1,0:T(8,128)}, s16[4,144,128]{2,1,0:T(8,128)(2,1)}, f32[16,128]{1,0:T(8,128)}) custom-call(s32[256]{0:T(256)} %bitcast.15, s32[256]{0:T(256)} %bitcast.14, s32[2]{0:T(128)} %bitcast.16, s32[2]{0:T(128)} %steps_s.3, s32[2,1,128]{2,1,0:T(1,128)} %cols_v.1, s32[16,128]{1,0:T(8,128)} %bitcast.12, ...), custom_call_target="tpu_custom_call" | custom-call | tf_op jit(solution)/shard_map/descent/pallas_call | solution.py:443
  43.8 4.4 %finish.1 = (f32[2048,128]{1,0:T(8,128)}, f32[2048,128]{1,0:T(8,128)}, f32[16,128]{1,0:T(8,128)}) custom-call(s32[2]{0:T(128)} %steps_s.3, f32[16,128]{1,0:T(8,128)} %get-tuple-element.10.dual_in, f32[2048,128]{1,0:T(8,128)} %get-tuple-element.11.mid_weights, f32[2048,128]{1,0:T(8,128)} %get-tuple-element.12.mid_sums, s16[4,144,128]{2,1,0:T(8,128)(2,1)} %get-tuple-element.13.near), custom_call_target="tpu_custom_call" | custom-call | tf_op jit(solution)/shard_map/finish/pallas_call | solution.py:492

commit v3 on v2

--- a/solution.py
+++ b/solution.py
@@ -120,12 +120,16 @@
     asked_s,
     answer,
     answered,
+    answer_sums,
+    answer_code,
+    answered_code,
     hrows,
     scaled,
     grads,
     coded,
     near0,
     far0,
+    quarter,
     codes,
     old,
     terms,
@@ -163,6 +167,14 @@
             tile_sem.at[section, load],
         )
 
+    def quarter_copy(which):
+        at = pl.multiple_of(q * QUARTER, QUARTER)
+        return pltpu.make_async_copy(
+            (weights_h, sums_h)[which].at[pl.ds(at, QUARTER)], quarter.at[which], local_sem.at[3 + which]
+        )
+
+    for which in range(2):
+        quarter_copy(which).start()
     copy_w = pltpu.make_async_copy(weights_h, weights, local_sem.at[0])
     copy_w.start()
     for load in range(LOADS[0]):
@@ -272,21 +284,24 @@
             jnp.int16
         )
 
+    for which in range(2):
+        quarter_copy(which).wait()
+    for piece in range(PIECES):
+        codes[piece, 0] = encode_log(quarter[0, pl.ds(piece * PIECE, PIECE), :], WEIGHT_CODE)
+        codes[piece, 1] = encode_sums(quarter[1, pl.ds(piece * PIECE, PIECE), :])
+    pl.semaphore_wait(barrier, len(senders))
+    ask.start()
+    dense(0, 0).start()
+    dense(0, 1).start()
     copy_w.wait()
     margins = forward(0, lambda k: weights[pl.ds(cols_s[k], 1), :])
     logits = new_logits(0, dual_v[...], margins)
 
-    pl.semaphore_wait(barrier, len(senders))
-    ask.start()
+    copy_s.wait()
     backward(0)
     for way in range(2):
         grad(0, 0, way).start()
 
-    copy_s.wait()
-    for piece in range(PIECES):
-        at = pl.multiple_of(q * QUARTER + piece * PIECE, PIECE)
-        codes[piece, 0] = encode_log(weights[pl.ds(at, PIECE), :], WEIGHT_CODE)
-        codes[piece, 1] = encode_sums(sums[pl.ds(at, PIECE), :])
     coded[0, :SLOTS, :] = encode_log(grads[0, :SLOTS, :], GRADIENT_CODE)
 
     ask.wait()
@@ -298,47 +313,49 @@
         for j in range(GROUP):
             k = g * GROUP + j
             at = asked_s[0, k]
-            answer[0, pl.ds(k, 1), :] = weights[pl.ds(at, 1), :]
-            answer[1, pl.ds(k, 1), :] = sums[pl.ds(at, 1), :]
+            answer[pl.ds(k, 1), :] = weights[pl.ds(at, 1), :]
+            answer_sums[pl.ds(k, 1), :] = sums[pl.ds(at, 1), :]
         return carry
 
     lax.fori_loop(0, GROUPS, gather, 0)
+    answer_code[...] = encode_sums(answer_sums[...])
     give = remote(answer, answered, answer_sem.at[0], answer_sem.at[1], (after, q))
     give.start()
-    for piece in range(PIECES):
-        dense(0, piece).start()
-    for way in range(2):
-        grad(2, 0, way).start()
-
+    give_sums = remote(answer_code, answered_code, answer_sem.at[2], answer_sem.at[3], (after, q))
+    give_sums.start()
+
+    dense_arrived(0, 0)
+    dense(1, 0).start()
+    dense(2, 0).start()
     mine = jnp.transpose(jnp.broadcast_to(cols_v[1].astype(F32), (TILE, TILE)))
     mine = jnp.concatenate([mine] * SUBS, axis=1)
     for way in range(2):
         grad_arrived(0, 0, way)
         grad(0, 1, way).start()
+    dense_arrived(0, 1)
+    dense(1, 1).start()
+    dense(2, 1).start()
     give.wait_recv()
+    give_sums.wait_recv()
+    answered_sums = decode_sums(answered_code[...])
     for way in range(2):
         grad_arrived(0, 1, way)
+    for way in range(2):
+        grad(2, 0, way).start()
     fill_terms(terms, near0, False)
     picked = onehot_sum(mine == lane_ids(near0, False), terms[...])
-    gradient = PENALTY * answered[0] + picked
-    after_sums = answered[1] + gradient * gradient
-    hrows[...] = answered[0] - primal_step(steps_s, 0, (SLOTS, TILE)) * gradient / jnp.sqrt(after_sums)
+    gradient = PENALTY * answered[...] + picked
+    after_sums = answered_sums + gradient * gradient
+    hrows[...] = answered[...] - primal_step(steps_s, 0, (SLOTS, TILE)) * gradient / jnp.sqrt(after_sums)
 
     margins = forward(1, lambda k: hrows[pl.ds(k, 1), :])
     logits = new_logits(1, logits, margins)
     dual_out[...] = logits
-    dense_arrived(0, 0)
-    dense(1, 0).start()
-    dense(2, 0).start()
     backward(1)
     coded[1, :SLOTS, :] = encode_log(grads[1, :SLOTS, :], GRADIENT_CODE)
     for way in range(2):
         grad(1, 0, way).start()
 
-    for piece in range(1, PIECES):
-        dense_arrived(0, piece)
-        dense(1, piece).start()
-        dense(2, piece).start()
     for way in range(2):
         grad_arrived(2, 0, way)
         grad(2, 1, way).start()
@@ -396,6 +413,7 @@
             for way in range(2):
                 grad(kind, stage, way).wait_send()
     give.wait_send()
+    give_sums.wait_send()
     for owner in range(SUBS):
         for which in range(2):
             mid_copy(owner, which).wait()
@@ -451,22 +469,26 @@
             pltpu.VMEM((CTILES, TILE), F32),
             pltpu.VMEM((1, SLOTS), I32),
             pltpu.SMEM((1, SLOTS), I32),
-            pltpu.VMEM((2, SLOTS, TILE), F32),
-            pltpu.VMEM((2, SLOTS, TILE), F32),
+            pltpu.VMEM((SLOTS, TILE), F32),
+            pltpu.VMEM((SLOTS, TILE), F32),
+            pltpu.VMEM((SLOTS, TILE), F32),
+            pltpu.VMEM((SLOTS, TILE), jnp.int16),
+            pltpu.VMEM((SLOTS, TILE), jnp.int16),
             pltpu.VMEM((SLOTS, TILE), F32),
             pltpu.VMEM((GROUP, TILE), F32),
             pltpu.VMEM((2, GROWS, TILE), F32),
             pltpu.VMEM((2, CROWS, TILE), jnp.int16),
             pltpu.VMEM((SUBS, GROWS, TILE), F32),
             pltpu.VMEM((SUBS, CROWS, TILE), jnp.int16),
+            pltpu.VMEM((2, QUARTER, TILE), F32),
             pltpu.VMEM((PIECES, 2, PIECE, TILE), jnp.int16),
             pltpu.VMEM((SUBS, PIECES, 2, PIECE, TILE), jnp.int16),
             pltpu.VMEM((SUBS * SLOTS, 2 * TILE), BF16),
             pltpu.VMEM((2, CTILES, TILE), F32),
             dma((2, max(LOADS))),
-            dma((3,)),
+            dma((5,)),
             dma((2,)),
-            dma((2,)),
+            dma((4,)),
             dma((4, PIECES)),
             dma((4, PIECES)),
             dma((3, 2, 2)),

time: 48.3 us -> 41.8 us (0.87)
  Pallas kernels: 47.5 us -> 41 us
    pallas_call x1, Pallas kernels: 43.1 us -> 36.6 us  [per_device(): pl.pallas_call(functools.partial(kernel, n), out_shape=(dense_shape, dens...]
where the time goes in v3:
time: 41.8 us; the launch traced here: 41.6 us
  Pallas kernels  41 us (98%)
  between operations  0.64 us (2%)
    pallas_call x1, Pallas kernels, per_device(): pl.pallas_call(functools.partial(kernel, n), out_shape=(dense_shape, dens...  36.6 us
    pallas_call x1, Pallas kernels, per_device(): pl.pallas_call(finish_kernel, out_shape=(dense_shape, dense_shape, row_sh...  4.39 us

profile of v3, /device:TPU:1, one launch (start us, length us, event | category | flops | bytes accessed | tf_op | source)
XLA Modules:
  0.0 41.6 jit_solution(4045825143913716169)
XLA Ops:
  0.6 36.6 %descent.1 = (f32[2048,128]{1,0:T(8,128)}, f32[2048,128]{1,0:T(8,128)}, s16[4,144,128]{2,1,0:T(8,128)(2,1)}, f32[16,128]{1,0:T(8,128)}) custom-call(s32[256]{0:T(256)} %bitcast.15, s32[256]{0:T(256)} %bitcast.14, s32[2]{0:T(128)} %bitcast.16, s32[2]{0:T(128)} %steps_s.3, s32[2,1,128]{2,1,0:T(1,128)} %cols_v.1, s32[16,128]{1,0:T(8,128)} %bitcast.12, ...), custom_call_target="tpu_custom_call" | custom-call | tf_op jit(solution)/shard_map/descent/pallas_call | solution.py:461
  37.2 4.4 %finish.1 = (f32[2048,128]{1,0:T(8,128)}, f32[2048,128]{1,0:T(8,128)}, f32[16,128]{1,0:T(8,128)}) custom-call(s32[2]{0:T(128)} %steps_s.3, f32[16,128]{1,0:T(8,128)} %get-tuple-element.10.dual_in, f32[2048,128]{1,0:T(8,128)} %get-tuple-element.11.mid_weights, f32[2048,128]{1,0:T(8,128)} %get-tuple-element.12.mid_sums, s16[4,144,128]{2,1,0:T(8,128)(2,1)} %get-tuple-element.13.near), custom_call_target="tpu_custom_call" | custom-call | tf_op jit(solution)/shard_map/finish/pallas_call | solution.py:514

commit v4 on v3

--- a/solution.py
+++ b/solution.py
@@ -22,7 +22,7 @@
 CROWS = SLOTS + GROUP
 OUT_PARTS = SUBS
 OUT_PART = CTILES // OUT_PARTS
-LOADS = (4, 2)
+LOADS = (4, 1)
 
 PENALTY = 0.1
 DUAL_RATE = 0.5
@@ -142,6 +142,8 @@
     dense_recv,
     grad_send,
     grad_recv,
+    last_send,
+    last_recv,
     out_sem,
 ):
     p = lax.axis_index("blk")
@@ -155,7 +157,7 @@
     before2 = lax.rem(p + n - 2, n)
 
     barrier = pltpu.get_barrier_semaphore()
-    senders = [(before, q), (before, opp), (before2, q), (before2, opp), (after, q), (p, twin), (p, opp)]
+    senders = [(before, q), (before, opp), (before, twin), (before, opptwin), (before2, q), (before2, opp), (after, q), (p, twin), (p, opp)]
     for device in senders:
         pl.semaphore_signal(barrier, inc=1, device_id=device, device_id_type=MESH)
 
@@ -278,6 +280,16 @@
             ref, ref, grad_send.at[kind, stage, way], grad_recv.at[kind, stage, way], (p, twin)
         ).wait_recv()
 
+    def last(turn):
+        to = (q, opp, twin, opptwin)[turn]
+        return remote(
+            coded.at[1], near1.at[q], last_send.at[turn], last_recv.at[turn], (after, to)
+        )
+
+    def last_arrived(turn):
+        ref = near1.at[(q, opp, twin, opptwin)[turn]]
+        remote(ref, ref, last_send.at[turn], last_recv.at[turn], (p, twin)).wait_recv()
+
     grads[0, pl.ds(SLOTS, 8), :] = jnp.broadcast_to(cols_v[0].astype(F32), (8, TILE))
     for section in range(2):
         coded[section, pl.ds(SLOTS, GROUP), :] = jnp.broadcast_to(cols_v[section], (GROUP, TILE)).astype(
@@ -286,12 +298,15 @@
 
     for which in range(2):
         quarter_copy(which).wait()
-    for piece in range(PIECES):
+    def encode(piece):
         codes[piece, 0] = encode_log(quarter[0, pl.ds(piece * PIECE, PIECE), :], WEIGHT_CODE)
         codes[piece, 1] = encode_sums(quarter[1, pl.ds(piece * PIECE, PIECE), :])
+
+    encode(0)
     pl.semaphore_wait(barrier, len(senders))
     ask.start()
     dense(0, 0).start()
+    encode(1)
     dense(0, 1).start()
     copy_w.wait()
     margins = forward(0, lambda k: weights[pl.ds(cols_s[k], 1), :])
@@ -301,8 +316,10 @@
     backward(0)
     for way in range(2):
         grad(0, 0, way).start()
-
     coded[0, :SLOTS, :] = encode_log(grads[0, :SLOTS, :], GRADIENT_CODE)
+    for way in range(2):
+        grad(2, 0, way).start()
+
 
     ask.wait()
     to_scalar = pltpu.make_async_copy(asked_v, asked_s, local_sem.at[2])
@@ -340,8 +357,6 @@
     answered_sums = decode_sums(answered_code[...])
     for way in range(2):
         grad_arrived(0, 1, way)
-    for way in range(2):
-        grad(2, 0, way).start()
     fill_terms(terms, near0, False)
     picked = onehot_sum(mine == lane_ids(near0, False), terms[...])
     gradient = PENALTY * answered[...] + picked
@@ -351,14 +366,14 @@
     margins = forward(1, lambda k: hrows[pl.ds(k, 1), :])
     logits = new_logits(1, logits, margins)
     dual_out[...] = logits
-    backward(1)
-    coded[1, :SLOTS, :] = encode_log(grads[1, :SLOTS, :], GRADIENT_CODE)
-    for way in range(2):
-        grad(1, 0, way).start()
-
     for way in range(2):
         grad_arrived(2, 0, way)
         grad(2, 1, way).start()
+    backward(1)
+    coded[1, :SLOTS, :] = encode_log(grads[1, :SLOTS, :], GRADIENT_CODE)
+    for turn in range(SUBS):
+        last(turn).start()
+
     dense_arrived(1, 0)
     dense(3, 0).start()
     for way in range(2):
@@ -394,29 +409,27 @@
     for piece in range(1, PIECES):
         dense_arrived(1, piece)
         dense(3, piece).start()
-    for way in range(2):
-        grad_arrived(1, 0, way)
-        grad(1, 1, way).start()
     section0(opp)
     for piece in range(PIECES):
         dense_arrived(3, piece)
     section0(opptwin)
 
-    for way in range(2):
-        grad_arrived(1, 1, way)
-
     for stage in range(4):
         for piece in range(PIECES):
             dense(stage, piece).wait_send()
-    for kind in range(3):
+    for kind in (0, 2):
         for stage in range(2):
             for way in range(2):
                 grad(kind, stage, way).wait_send()
     give.wait_send()
     give_sums.wait_send()
+    for turn in range(SUBS):
+        last(turn).wait_send()
     for owner in range(SUBS):
         for which in range(2):
             mid_copy(owner, which).wait()
+    for turn in range(SUBS):
+        last_arrived(turn)
 
 
 def finish_kernel(
@@ -493,6 +506,8 @@
             dma((4, PIECES)),
             dma((3, 2, 2)),
             dma((3, 2, 2)),
+            dma((SUBS,)),
+            dma((SUBS,)),
             dma((2, OUT_PARTS)),
         ],
         compiler_params=pltpu.CompilerParams(

time: 41.8 us -> 40.4 us (0.967)
  Pallas kernels: 41 us -> 39.6 us
    pallas_call x1, Pallas kernels: 36.6 us -> 35.3 us  [per_device(): pl.pallas_call(functools.partial(kernel, n), out_shape=(dense_shape, dens...]
where the time goes in v4:
time: 40.4 us; the launch traced here: 40.3 us
  Pallas kernels  39.6 us (98%)
  between operations  0.64 us (2%)
    pallas_call x1, Pallas kernels, per_device(): pl.pallas_call(functools.partial(kernel, n), out_shape=(dense_shape, dens...  35.3 us
    pallas_call x1, Pallas kernels, per_device(): pl.pallas_call(finish_kernel, out_shape=(dense_shape, dense_shape, row_sh...  4.4 us

profile of v4, /device:TPU:1, one launch (start us, length us, event | category | flops | bytes accessed | tf_op | source)
XLA Modules:
  0.0 40.3 jit_solution(16165890472374730325)
XLA Ops:
  0.6 35.3 %descent.1 = (f32[2048,128]{1,0:T(8,128)}, f32[2048,128]{1,0:T(8,128)}, s16[4,144,128]{2,1,0:T(8,128)(2,1)}, f32[16,128]{1,0:T(8,128)}) custom-call(s32[256]{0:T(256)} %bitcast.15, s32[256]{0:T(256)} %bitcast.14, s32[2]{0:T(128)} %bitcast.16, s32[2]{0:T(128)} %steps_s.3, s32[2,1,128]{2,1,0:T(1,128)} %cols_v.1, s32[16,128]{1,0:T(8,128)} %bitcast.12, ...), custom_call_target="tpu_custom_call" | custom-call | tf_op jit(solution)/shard_map/descent/pallas_call | solution.py:474
  35.9 4.4 %finish.1 = (f32[2048,128]{1,0:T(8,128)}, f32[2048,128]{1,0:T(8,128)}, f32[16,128]{1,0:T(8,128)}) custom-call(s32[2]{0:T(128)} %steps_s.3, f32[16,128]{1,0:T(8,128)} %get-tuple-element.10.dual_in, f32[2048,128]{1,0:T(8,128)} %get-tuple-element.11.mid_weights, f32[2048,128]{1,0:T(8,128)} %get-tuple-element.12.mid_sums, s16[4,144,128]{2,1,0:T(8,128)(2,1)} %get-tuple-element.13.near), custom_call_target="tpu_custom_call" | custom-call | tf_op jit(solution)/shard_map/finish/pallas_call | solution.py:529
